TPU v7x, 32 devices: a whole 2x2x4 slice. The times are simulated.
32 devices in a mesh: row: 8 (over z, core), col: 4 (over y, x).
Axes of the slice: x: 2, y: 2, z: 4, core: 2. Of those that a mesh axis runs over, the one named last changes fastest.
Arguments:
- tokens: bfloat16 [128, 8192], P('row', 'col'), may hold values from -6 to 6
- out_grad: bfloat16 [128, 8192], P('row', 'col'), may hold values from -1.5 to 1.5
- gate_weight: bfloat16 [8192, 16384], P('col', 'row'), may hold values from -0.0625 to 0.0625
- up_weight: bfloat16 [8192, 16384], P('col', 'row'), may hold values from -0.0625 to 0.0625
- down_weight: bfloat16 [16384, 8192], P('row', 'col'), may hold values from -0.046875 to 0.046875
Outputs:
- input_grad: bfloat16 [128, 8192], P('row', 'col')
- gate_weight_grad: bfloat16 [8192, 16384], P('col', 'row')
- up_weight_grad: bfloat16 [8192, 16384], P('col', 'row')
- down_weight_grad: bfloat16 [16384, 8192], P('row', 'col')
All inputs are finite; a program needn't handle non-finite values.
Results may differ from a plain program's by a relative error of at most 0.005.
Values may be sent and summed in bfloat16 or wider, within the bound.
A program may use at most 128 MiB of HBM per device.

v0:
```python
import jax
import jax.numpy as jnp
from jax import lax
from jax.sharding import PartitionSpec as P


def pointwise(gate, up, hidden_grad):
    sig = jax.nn.sigmoid(gate)
    act = gate * sig
    hidden = (act * up).astype(jnp.bfloat16)
    gate_grad = (hidden_grad * up * sig * (1.0 + gate * (1.0 - sig))).astype(jnp.bfloat16)
    up_grad = (hidden_grad * act).astype(jnp.bfloat16)
    return (hidden, gate_grad, up_grad)


def body(tokens, out_grad, gate_weight, up_weight, down_weight):
    rows_all, grads_all = (
        lax.all_gather(tokens, "row", axis=0, tiled=True),
        lax.all_gather(out_grad, "row", axis=0, tiled=True),
    )
    contract_cols = (((1,), (1,)), ((), ()))
    contract_rows = (((0,), (0,)), ((), ()))
    gate_part = jnp.dot(rows_all, gate_weight, preferred_element_type=jnp.float32)
    up_part = jnp.dot(rows_all, up_weight, preferred_element_type=jnp.float32)
    grad_part = lax.dot_general(
        grads_all, down_weight, contract_cols, preferred_element_type=jnp.float32
    )
    gate, up, hidden_grad = lax.psum((gate_part, up_part, grad_part), "col")
    hidden, gate_grad, up_grad = pointwise(gate, up, hidden_grad)
    gate_weight_grad = lax.dot_general(
        rows_all, gate_grad, contract_rows, preferred_element_type=jnp.float32
    ).astype(jnp.bfloat16)
    up_weight_grad = lax.dot_general(
        rows_all, up_grad, contract_rows, preferred_element_type=jnp.float32
    ).astype(jnp.bfloat16)
    down_weight_grad = lax.dot_general(
        hidden, grads_all, contract_rows, preferred_element_type=jnp.float32
    ).astype(jnp.bfloat16)
    total = lax.dot_general(
        gate_grad, gate_weight, contract_cols, preferred_element_type=jnp.float32
    )
    input_grad = lax.psum_scatter(
        total
        + lax.dot_general(up_grad, up_weight, contract_cols, preferred_element_type=jnp.float32),
        "row",
        scatter_dimension=0,
        tiled=True,
    )
    return (input_grad.astype(jnp.bfloat16), gate_weight_grad, up_weight_grad, down_weight_grad)


def solution(mesh):
    return jax.shard_map(
        body,
        mesh=mesh,
        in_specs=(
            P("row", "col"),
            P("row", "col"),
            P("col", "row"),
            P("col", "row"),
            P("row", "col"),
        ),
        out_specs=(P("row", "col"), P("col", "row"), P("col", "row"), P("row", "col")),
        check_vma=False,
    )
```

profile of v0, /device:TPU:0, one launch (start us, length us, event | category | flops | bytes accessed | tf_op | source)
XLA Modules:
  0.0 206.5 jit_solution(15775677043860915779)
XLA Ops:
  7.2 0.0 all-reduce.3.cloned.1.call-start
  7.2 0.0 slice-start
  7.2 16.9 %all_gather.7 = bf16[128,2048]{1,0:T(8,128)(2,1)S(1)} all-gather(bf16[16,2048]{1,0:T(8,128)(2,1)} %param.5), channel_id=1, replica_groups=mesh['row'=8,'col'=4] {'row'}, dimensions={0}, use_global_device_ids=true | all-gather | bytes 589824 | tf_op jit(solution)/shard_map/all_gather | solution.py:18
  24.1 14.9 %all_gather.6 = bf16[128,2048]{1,0:T(8,128)(2,1)S(1)} all-gather(bf16[16,2048]{1,0:T(8,128)(2,1)} %param.6), channel_id=1, replica_groups=mesh['row'=8,'col'=4] {'row'}, dimensions={0}, use_global_device_ids=true | all-gather | bytes 589824 | tf_op jit(solution)/shard_map/all_gather | solution.py:19
  39.1 0.0 slice-start.1
  39.1 0.0 slice-start.2
  39.1 5.8 %fusion.5 = f32[128,2048]{1,0:T(8,128)} fusion(bf16[128,2048]{1,0:T(8,128)(2,1)S(1)} %all_gather.7, bf16[2048,2048]{1,0:T(8,128)(2,1)} %param.7), kind=kOutput, calls=%fused_computation.12 | convolution fusion | flops 1073741824 | bytes 9961472 | tf_op jit(solution)/shard_map/dot_general | solution.py:23
  44.8 0.0 slice-done
  44.8 0.0 slice-done.1
  44.8 0.0 slice-start.3
  44.9 2.3 %fusion.4 = f32[128,2048]{1,0:T(8,128)} fusion(bf16[128,2048]{1,0:T(8,128)(2,1)S(1)} %all_gather.7, bf16[2048,2048]{1,0:T(8,128)(2,1)S(1)} %bitcast.20), kind=kOutput, calls=%fused_computation.11 | convolution fusion | flops 1073741824 | bytes 9961472 | tf_op jit(solution)/shard_map/dot_general | solution.py:24
  47.1 0.0 slice-done.2
  47.1 0.0 slice-done.3
  47.1 3.9 %fusion.3 = f32[128,2048]{1,0:T(8,128)} fusion(bf16[128,2048]{1,0:T(8,128)(2,1)S(1)} %all_gather.6, bf16[2048,2048]{1,0:T(8,128)(2,1)S(1)} %bitcast.22), kind=kOutput, calls=%fused_computation.10 | convolution fusion | flops 1073741824 | bytes 9961472 | tf_op jit(solution)/shard_map/dot_general | solution.py:25
  51.0 0.0 all-reduce.3.cloned.1.call-update
  51.0 0.2 reduce-scatter.2.cloned.1.call-start
  51.2 89.0 %all-reduce.3.cloned.1.call-done = (f32[128,2048]{1,0:T(8,128)}, f32[128,2048]{1,0:T(8,128)}, f32[128,2048]{1,0:T(8,128)}) async-done(((f32[128,2048]{1,0:T(8,128)}, f32[128,2048]{1,0:T(8,128)}, f32[128,2048]{1,0:T(8,128)}), (f32[128,2048]{1,0:T(8,128)}, f32[128,2048]{1,0:T(8,128)}, f32[128,2048]{1,0:T(8,128)})) %all-reduce.3.cloned.1.call-update) | async-done | bytes 3145744 | tf_op jit(solution)/shard_map/psum | solution.py:28
  140.2 2.4 %multiply_convert_fusion.1 = (bf16[128,2048]{1,0:T(8,128)(2,1)S(1)}, bf16[128,2048]{1,0:T(8,128)(2,1)S(1)}) fusion(f32[128,2048]{1,0:T(8,128)} %get-tuple-element.9, f32[128,2048]{1,0:T(8,128)} %get-tuple-element.8, f32[128,2048]{1,0:T(8,128)} %get-tuple-element.10), kind=kLoop, calls=%fused_computation.5 | loop fusion | flops 3407872 | bytes 4194304 | tf_op jit(solution)/shard_map/convert_element_type | solution.py:12
  142.6 6.3 %fusion.6 = f32[128,2048]{1,0:T(8,128)S(1)} fusion(bf16[128,2048]{1,0:T(8,128)(2,1)S(1)} %get-tuple-element.12, bf16[2048,2048]{1,0:T(8,128)(2,1)} %param.7), kind=kOutput, calls=%fused_computation.13 | convolution fusion | flops 1073741824 | bytes 9961472 | tf_op jit(solution)/shard_map/dot_general | solution.py:39
  148.9 7.3 %convolution_add_fusion = f32[128,2048]{1,0:T(8,128)} fusion(f32[128,2048]{1,0:T(8,128)S(1)} %fusion.6, bf16[128,2048]{1,0:T(8,128)(2,1)S(1)} %get-tuple-element.11, bf16[2048,2048]{1,0:T(8,128)(2,1)} %param.8), kind=kOutput, calls=%fused_computation.3 | convolution fusion | flops 1074003968 | bytes 11010048 | tf_op jit(solution)/shard_map/dot_general | solution.py:44
  156.2 0.0 reduce-scatter.2.cloned.1.call-update
  156.2 5.8 %convert_bitcast_fusion.1 = bf16[2048,2048]{0,1:T(8,128)(2,1)} fusion(bf16[128,2048]{1,0:T(8,128)(2,1)S(1)} %get-tuple-element.12, bf16[128,2048]{1,0:T(8,128)(2,1)S(1)} %all_gather.7), kind=kOutput, calls=%fused_computation.1 | convolution fusion | flops 1077936128 | bytes 9437184 | tf_op jit(solution)/shard_map/dot_general | solution.py:30
  162.0 12.2 %copy.9 = bf16[2048,2048]{1,0:T(8,128)(2,1)} copy(bf16[2048,2048]{0,1:T(8,128)(2,1)} %convert_bitcast_fusion.1) | data formatting | bytes 16777216
  174.2 5.8 %convert_bitcast_fusion = bf16[2048,2048]{0,1:T(8,128)(2,1)} fusion(bf16[128,2048]{1,0:T(8,128)(2,1)S(1)} %get-tuple-element.11, bf16[128,2048]{1,0:T(8,128)(2,1)S(1)} %all_gather.7), kind=kOutput, calls=%fused_computation | convolution fusion | flops 1077936128 | bytes 9437184 | tf_op jit(solution)/shard_map/dot_general | solution.py:33
  180.0 0.0 copy-start
  180.0 0.0 copy-start.1
  180.0 12.4 %copy.10 = bf16[2048,2048]{1,0:T(8,128)(2,1)} copy(bf16[2048,2048]{0,1:T(8,128)(2,1)} %convert_bitcast_fusion) | data formatting | bytes 16777216
  192.4 0.0 copy-done
  192.4 0.0 copy-done.1
  192.4 5.8 %convolution_convert_fusion = bf16[2048,2048]{1,0:T(8,128)(2,1)} fusion(bf16[128,2048]{1,0:T(8,128)(2,1)S(1)} %all_gather.6, f32[128,2048]{1,0:T(8,128)S(1)} %copy-done.1, f32[128,2048]{1,0:T(8,128)S(1)} %copy-done), kind=kOutput, calls=%fused_computation.2 | convolution fusion | flops 1079508992 | bytes 11010048 | tf_op jit(solution)/shard_map/dot_general | solution.py:36
  198.2 0.0 reduce-scatter.2.cloned.1.call-done
  198.2 1.5 convert_element_type.29
  (2 shorter events, 0.0 us)
Async XLA Ops:
  7.2 133.0 %all-reduce.3.cloned.1.call-start = ((), (), s32[]{:S(2)}) async-start(), calls=%async_computation.2 | async-start | bytes 6291456 | tf_op jit(solution)/shard_map/psum | solution.py:28
  7.2 37.6 %slice-start = ((s8[8388608]{0:T(1024)(128)(4,1)}), s8[4194304]{0:T(1024)(128)(4,1)S(1)}, s32[]{:S(2)}) async-start(s8[8388608]{0:T(1024)(128)(4,1)} %bitcast.19), calls=%async_computation.3 | async-start | bytes 8388608
  39.1 5.8 %slice-start.1 = ((s8[8388608]{0:T(1024)(128)(4,1)}), s8[4194304]{0:T(1024)(128)(4,1)S(1)}, s32[]{:S(2)}) async-start(s8[8388608]{0:T(1024)(128)(4,1)} %bitcast.19), calls=%async_computation.4 | async-start | bytes 8388608
  39.1 8.0 %slice-start.2 = ((s8[8388608]{0:T(1024)(128)(4,1)}), s8[4194304]{0:T(1024)(128)(4,1)S(1)}, s32[]{:S(2)}) async-start(s8[8388608]{0:T(1024)(128)(4,1)} %bitcast.21), calls=%async_computation.5 | async-start | bytes 8388608
  44.8 2.3 %slice-start.3 = ((s8[8388608]{0:T(1024)(128)(4,1)}), s8[4194304]{0:T(1024)(128)(4,1)S(1)}, s32[]{:S(2)}) async-start(s8[8388608]{0:T(1024)(128)(4,1)} %bitcast.21), calls=%async_computation.6 | async-start | bytes 8388608
  51.0 147.2 %reduce-scatter.2.cloned.1.call-start = ((), (), s32[]{:S(2)}) async-start(), calls=%async_computation.1 | async-start | bytes 1179648 | tf_op jit(solution)/shard_map/reduce_scatter | solution.py:42
  180.0 12.4 %copy-start = (f32[128,2048]{1,0:T(8,128)S(1)}, f32[128,2048]{1,0:T(8,128)}, u32[]{:S(2)}) copy-start(f32[128,2048]{1,0:T(8,128)} %get-tuple-element.8) | copy-start | bytes 3145732
  180.0 12.4 %copy-start.1 = (f32[128,2048]{1,0:T(8,128)S(1)}, f32[128,2048]{1,0:T(8,128)}, u32[]{:S(2)}) copy-start(f32[128,2048]{1,0:T(8,128)} %get-tuple-element.10) | copy-start | bytes 3145732
Sparse Core Ops, SparseCore 0:
  51.1 89.0 all-reduce.2
  156.3 32.4 reduce-scatter.1
where the time goes:
time: 207 us
  waiting for transfers between devices  89 us (43%)
  matrix products  42.8 us (21%)
  blocking collectives  31.9 us (15%)
  local copies, waits for them, and re-layouts  24.7 us (12%)
  between operations  14.1 us (7%)
  other arithmetic  3.95 us (2%)
    psum x1, waiting for transfers between devices, body(): gate, up, hidden_grad = lax.psum((gate_part, up_part, grad_part), 'col')  89 us
    unnamed x14, local copies, waits for them, and re-layouts  24.7 us
    all_gather x1, blocking collectives, body(): lax.all_gather(tokens, 'row', axis=0, tiled=True)  16.9 us
    all_gather x1, blocking collectives, body(): lax.all_gather(out_grad, 'row', axis=0, tiled=True)  14.9 us
    dot_general x1, matrix products, body(): lax.dot_general(up_grad, up_weight, contract_cols, preferred_element_type...  7.27 us
    dot_general x1, matrix products, body(): lax.dot_general(gate_grad, gate_weight, contract_cols, preferred_element_...  6.26 us
    dot_general x1, matrix products, body(): lax.dot_general(hidden, grads_all, contract_rows, preferred_element_type=...  5.8 us
    dot_general x1, matrix products, body(): lax.dot_general(rows_all, gate_grad, contract_rows, preferred_element_typ...  5.77 us
  transfers between devices with their start and end apart: 2, of which 1 were waited for; matrix products, arithmetic and copies ran while one was open for 20% of the time, Pallas kernels for 0%

commit v1 on v0

v1 whole, which is shorter than its diff:
```python
import functools

import jax
import jax.numpy as jnp
from jax import lax
from jax.experimental import pallas as pl
from jax.experimental.pallas import tpu as pltpu
from jax.sharding import PartitionSpec as P

F32, BF16 = jnp.float32, jnp.bfloat16
MESH = pl.DeviceIdType.MESH
NN = (((1,), (0,)), ((), ()))
NT = (((1,), (1,)), ((), ()))
TN = (((0,), (0,)), ((), ()))


def mm(a, b, dims):
    return lax.dot_general(a, b, dims, preferred_element_type=F32)


def xor(a, b, n):
    out, bit = 0, 1
    while bit < n:
        out = out + lax.rem(a // bit + (b // bit) % 2, 2) * bit
        bit *= 2
    return out


def layer_kernel(
    nrow, ncol,
    tok_ref, og_ref, gw_hbm, uw_hbm, dw_hbm,
    rows_hbm, grads_hbm, res_hbm, ig_ref,
    gw, uw, dw, rows, grads, part, wide, inbox, res, tot, sib, pair, pbox,
    w_sem, out_sem, g_send, g_recv, f_send, f_recv,
    rs_send, rs_recv, ag_send, ag_recv, s_send, s_recv, p_send, p_recv,
):
    nz = nrow // 2
    nc, d_loc, cw = gw.shape
    tb = tok_ref.shape[0]
    tc = rows.shape[0] // ncol
    r, me = lax.axis_index("row"), lax.axis_index("col")
    z, core = r // 2, lax.rem(r, 2)
    sibling = z * 2 + 1 - core

    def block(i, n):
        return pl.ds(pl.multiple_of(i * n, n), n)

    barrier = pltpu.get_barrier_semaphore()
    pl.semaphore_signal(barrier, inc=1, device_id={"row": sibling}, device_id_type=MESH)
    for k in range(1, nz):
        pl.semaphore_signal(barrier, inc=1, device_id={"row": xor(z, k, nz) * 2 + core}, device_id_type=MESH)
    for k in range(1, ncol):
        pl.semaphore_signal(barrier, inc=1, device_id={"col": xor(me, k, ncol)}, device_id_type=MESH)

    def weight_copy(i, c):
        cols = block(c, cw)
        src = dw_hbm.at[cols, :] if i == 2 else (gw_hbm, uw_hbm)[i].at[:, cols]
        return pltpu.make_async_copy(src, (gw, uw, dw)[i].at[c], w_sem.at[i, c])

    for c in range(nc):
        weight_copy(0, c).start()
        weight_copy(1, c).start()
    for c in range(nc):
        weight_copy(2, c).start()
    rows[block(r, tb), :] = tok_ref[...]
    grads[block(r, tb), :] = og_ref[...]
    pl.semaphore_wait(barrier, nz + ncol - 1)

    def gather_copy(a, k):
        buf = (rows, grads)[a]
        mine = buf.at[block(r, tb), :]
        to = sibling if k == 0 else xor(z, k, nz) * 2 + core
        return pltpu.make_async_remote_copy(
            mine, mine, g_send.at[a, k], g_recv.at[a, k], device_id={"row": to}, device_id_type=MESH
        )

    def forward_copy(a, k):
        buf = (rows, grads)[a]
        got = buf.at[block(xor(z, k, nz) * 2 + core, tb), :]
        return pltpu.make_async_remote_copy(
            got, got, f_send.at[a, k - 1], f_recv.at[a, k - 1], device_id={"row": sibling}, device_id_type=MESH
        )

    def finish_gather(a):
        for k in range(1, nz):
            gather_copy(a, k).wait_recv()
            forward_copy(a, k).start()
        gather_copy(a, 0).wait_recv()
        for k in range(1, nz):
            forward_copy(a, k).wait_recv()

    for a in range(2):
        for k in range(nz):
            gather_copy(a, k).start()

    def part_copy(c, kind, k):
        to = xor(me, k, ncol)
        which = pl.ds(0, 2) if kind == 0 else pl.ds(2, 1)
        return pltpu.make_async_remote_copy(
            part.at[c, which, block(to, tc), :], inbox.at[c, k - 1, which],
            rs_send.at[kind, c, k - 1], rs_recv.at[kind, c, k - 1],
            device_id={"col": to}, device_id_type=MESH,
        )

    out_rows = pltpu.make_async_copy(rows, rows_hbm, out_sem.at[0])
    out_grads = pltpu.make_async_copy(grads, grads_hbm, out_sem.at[1])
    out_res = pltpu.make_async_copy(res, res_hbm, out_sem.at[2])

    def keep(c, i, product):
        part[c, i] = product.astype(BF16)
        wide[c, i] = product

    finish_gather(0)
    out_rows.start()

    @pl.loop(0, nc)
    def _(c):
        for i, w in ((0, gw), (1, uw)):
            weight_copy(i, c).wait()
            keep(c, i, mm(rows[...], w[c], NN))
        for k in range(1, ncol):
            part_copy(c, 0, k).start()

    finish_gather(1)
    out_grads.start()

    @pl.loop(0, nc)
    def _(c):
        weight_copy(2, c).wait()
        keep(c, 2, mm(grads[...], dw[c], NT))
        for k in range(1, ncol):
            part_copy(c, 1, k).start()

    def res_copy(c, k):
        mine = res.at[c, :, block(me, tc), :]
        return pltpu.make_async_remote_copy(
            mine, mine, ag_send.at[c, k - 1], ag_recv.at[c, k - 1],
            device_id={"col": xor(me, k, ncol)}, device_id_type=MESH,
        )

    @pl.loop(0, nc)
    def _(c):
        own = block(me, tc)
        sums = [wide[c, i, own, :] for i in range(3)]
        for k in range(1, ncol):
            part_copy(c, 0, k).wait_recv()
            part_copy(c, 1, k).wait_recv()
            sums = [sums[i] + inbox[c, k - 1, i].astype(F32) for i in range(3)]
        gate, up, hidden_grad = sums
        sig = 1.0 / (1.0 + jnp.exp(-gate))
        act = gate * sig
        res[c, 0, own, :] = (act * up).astype(BF16)
        res[c, 1, own, :] = (hidden_grad * up * sig * (1.0 + gate * (1.0 - sig))).astype(BF16)
        res[c, 2, own, :] = (hidden_grad * act).astype(BF16)
        for k in range(1, ncol):
            res_copy(c, k).start()

    td = min(512, d_loc)
    tot[...] = jnp.zeros_like(tot)

    @pl.loop(0, nc)
    def _(c):
        for k in range(1, ncol):
            res_copy(c, k).wait_recv()
        for j in range(d_loc // td):
            cut = pl.ds(j * td, td)
            tot[:, cut] += mm(res[c, 1], gw[c, cut, :], NT) + mm(res[c, 2], uw[c, cut, :], NT)

    out_res.start()

    def sib_copy(k):
        return pltpu.make_async_remote_copy(
            tot.at[block(2 * k + 1 - core, tb), :], sib.at[k], s_send.at[k], s_recv.at[k],
            device_id={"row": sibling}, device_id_type=MESH,
        )

    def pair_copy(k):
        to = xor(z, k, nz)
        return pltpu.make_async_remote_copy(
            pair.at[to], pbox.at[k - 1], p_send.at[k - 1], p_recv.at[k - 1],
            device_id={"row": to * 2 + core}, device_id_type=MESH,
        )

    for k in range(nz):
        sib_copy(k).start()
    for k in range(nz):
        sib_copy(k).wait_recv()
    for k in range(nz):
        pair[k] = (tot[block(2 * k + core, tb), :] + sib[k]).astype(BF16)
    for k in range(1, nz):
        pair_copy(k).start()
    total = tot[block(r, tb), :] + sib[z]
    for k in range(1, nz):
        pair_copy(k).wait_recv()
        total = total + pbox[k - 1].astype(F32)
    ig_ref[...] = total.astype(BF16)

    for a in range(2):
        for k in range(nz):
            gather_copy(a, k).wait_send()
        for k in range(1, nz):
            forward_copy(a, k).wait_send()
    for k in range(1, ncol):
        @pl.loop(0, nc)
        def _(c):
            part_copy(c, 0, k).wait_send()
            part_copy(c, 1, k).wait_send()
            res_copy(c, k).wait_send()
    for k in range(nz):
        sib_copy(k).wait_send()
    for k in range(1, nz):
        pair_copy(k).wait_send()
    out_rows.wait()
    out_grads.wait()
    out_res.wait()


def layer(nrow, ncol, tokens, out_grad, gate_weight, up_weight, down_weight):
    tb, d_loc = tokens.shape
    ff = gate_weight.shape[1]
    t = tb * nrow
    cw = min(512, ff)
    nc, nz, tc = ff // cw, nrow // 2, t // ncol
    vmem = pl.BlockSpec(memory_space=pltpu.VMEM)
    hbm = pl.BlockSpec(memory_space=pl.ANY)
    dma = pltpu.SemaphoreType.DMA
    return pl.pallas_call(
        functools.partial(layer_kernel, nrow, ncol),
        out_shape=(
            jax.ShapeDtypeStruct((t, d_loc), BF16),
            jax.ShapeDtypeStruct((t, d_loc), BF16),
            jax.ShapeDtypeStruct((nc, 3, t, cw), BF16),
            jax.ShapeDtypeStruct((tb, d_loc), BF16),
        ),
        in_specs=[vmem, vmem, hbm, hbm, hbm],
        out_specs=(hbm, hbm, hbm, vmem),
        scratch_shapes=[
            pltpu.VMEM((nc, d_loc, cw), BF16),
            pltpu.VMEM((nc, d_loc, cw), BF16),
            pltpu.VMEM((nc, cw, d_loc), BF16),
            pltpu.VMEM((t, d_loc), BF16),
            pltpu.VMEM((t, d_loc), BF16),
            pltpu.VMEM((nc, 3, t, cw), BF16),
            pltpu.VMEM((nc, 3, t, cw), F32),
            pltpu.VMEM((nc, ncol - 1, 3, tc, cw), BF16),
            pltpu.VMEM((nc, 3, t, cw), BF16),
            pltpu.VMEM((t, d_loc), F32),
            pltpu.VMEM((nz, tb, d_loc), F32),
            pltpu.VMEM((nz, tb, d_loc), BF16),
            pltpu.VMEM((nz - 1, tb, d_loc), BF16),
            dma((3, nc)), dma((3,)),
            dma((2, nz)), dma((2, nz)), dma((2, nz - 1)), dma((2, nz - 1)),
            dma((2, nc, ncol - 1)), dma((2, nc, ncol - 1)),
            dma((nc, ncol - 1)), dma((nc, ncol - 1)),
            dma((nz,)), dma((nz,)), dma((nz - 1,)), dma((nz - 1,)),
        ],
        compiler_params=pltpu.CompilerParams(
            collective_id=0, has_side_effects=True, vmem_limit_bytes=48 * 1024 * 1024
        ),
        cost_estimate=pl.CostEstimate(
            flops=10 * t * d_loc * ff, bytes_accessed=6 * d_loc * ff, transcendentals=t * ff
        ),
    )(tokens, out_grad, gate_weight, up_weight, down_weight)


def grads_kernel(rows_ref, grads_ref, res_ref, hid_ref, gwg_ref, uwg_ref, dwg_ref):
    nc, _, _, cw = res_ref.shape
    for c in range(nc):
        cols = pl.ds(c * cw, cw)
        gwg_ref[:, cols] = mm(rows_ref[...], res_ref[c, 1], TN).astype(BF16)
        uwg_ref[:, cols] = mm(rows_ref[...], res_ref[c, 2], TN).astype(BF16)
    d_loc = grads_ref.shape[1]
    step = min(512, d_loc)
    for j in range(d_loc // step):
        cols = pl.ds(j * step, step)
        dwg_ref[:, cols] = mm(hid_ref[0, 0], grads_ref[:, cols], TN).astype(BF16)


def weight_grads(rows, grads, res):
    t, d_loc = rows.shape
    nc, _, _, cw = res.shape
    ff = nc * cw
    tile = min(256, cw)
    steps = ff // tile
    td = d_loc // steps
    per = cw // tile
    return pl.pallas_call(
        grads_kernel,
        grid=(steps,),
        out_shape=(
            jax.ShapeDtypeStruct((d_loc, ff), BF16),
            jax.ShapeDtypeStruct((d_loc, ff), BF16),
            jax.ShapeDtypeStruct((ff, d_loc), BF16),
        ),
        in_specs=[
            pl.BlockSpec((t, td), lambda i: (0, i)),
            pl.BlockSpec((t, d_loc), lambda i: (0, 0)),
            pl.BlockSpec((nc, 3, t, cw), lambda i: (0, 0, 0, 0)),
            pl.BlockSpec((1, 1, t, tile), lambda i: (i // per, 0, 0, i % per)),
        ],
        out_specs=(
            pl.BlockSpec((td, ff), lambda i: (i, 0)),
            pl.BlockSpec((td, ff), lambda i: (i, 0)),
            pl.BlockSpec((tile, d_loc), lambda i: (i, 0)),
        ),
        compiler_params=pltpu.CompilerParams(vmem_limit_bytes=32 * 1024 * 1024),
        cost_estimate=pl.CostEstimate(
            flops=6 * t * d_loc * ff, bytes_accessed=6 * d_loc * ff, transcendentals=0
        ),
    )(rows, grads, res, res)


def solution(mesh):
    nrow, ncol = mesh.shape["row"], mesh.shape["col"]

    def body(tokens, out_grad, gate_weight, up_weight, down_weight):
        rows, grads, res, input_grad = layer(
            nrow, ncol, tokens, out_grad, gate_weight, up_weight, down_weight
        )
        return (input_grad, *weight_grads(rows, grads, res))

    return jax.shard_map(
        body,
        mesh=mesh,
        in_specs=(
            P("row", "col"),
            P("row", "col"),
            P("col", "row"),
            P("col", "row"),
            P("row", "col"),
        ),
        out_specs=(P("row", "col"), P("col", "row"), P("col", "row"), P("row", "col")),
        check_vma=False,
    )
```

time: 207 us -> 78.1 us (0.38)
  waiting for transfers between devices: 89 us -> 0 us
  Pallas kernels: 0 us -> 74.9 us
  matrix products: 42.8 us -> 0 us
  blocking collectives: 31.9 us -> 0 us
  local copies, waits for them, and re-layouts: 24.7 us -> 2.3 us
  between operations: 14.1 us -> 0.65 us
  other arithmetic: 3.95 us -> 0 us
    psum x1 -> x0, waiting for transfers between devices: 89 us -> none  [body(): gate, up, hidden_grad = lax.psum((gate_part, up_part, grad_part), 'col')]
    pallas_call x0 -> x2, Pallas kernels: none -> 74.9 us  [the longest x1 64.3 us: layer(): pl.pallas_call(functools.partial(layer_kernel, nrow, ncol), out_shape=(ja...]
    dot_general x8 -> x0, matrix products: 42.8 us -> none  [the longest x1 7.27 us: body(): lax.dot_general(up_grad, up_weight, contract_cols, preferred_element_type...]
    all_gather x2 -> x0, blocking collectives: 31.9 us -> none  [the longest x1 16.9 us: body(): lax.all_gather(tokens, 'row', axis=0, tiled=True)]
    unnamed x14 -> x5, local copies, waits for them, and re-layouts: 24.7 us -> 2.3 us
    convert_element_type x2 -> x0, other arithmetic: 3.95 us -> none  [the longest x1 2.41 us: pointwise(): up_grad = (hidden_grad * act).astype(jnp.bfloat16)]
  transfers between devices with their start and end apart: 2 -> 0, of which waited for: 1 -> 0; matrix products, arithmetic and copies ran while one was open for 20% -> 0% of each run, Pallas kernels for 0% -> 0%
where the time goes in v1:
time: 78.1 us; the launch traced here: 77.9 us
  Pallas kernels  74.9 us (96%)
  local copies, waits for them, and re-layouts  2.3 us (3%)
    pallas_call x1, Pallas kernels, layer(): pl.pallas_call(functools.partial(layer_kernel, nrow, ncol), out_shape=(ja...  64.3 us
    pallas_call x1, Pallas kernels, weight_grads(): pl.pallas_call(grads_kernel, grid=(steps,), out_shape=(jax.ShapeDtypeStru...  10.6 us
    unnamed x5, local copies, waits for them, and re-layouts  2.3 us

profile of v1, /device:TPU:0, one launch (start us, length us, event | category | flops | bytes accessed | tf_op | source)
XLA Modules:
  0.0 77.9 jit_solution(13557441866906687819)
XLA Ops:
  0.6 0.0 copy-start
  0.6 0.8 %copy-done = bf16[16,2048]{1,0:T(8,128)(2,1)S(1)} copy-done((bf16[16,2048]{1,0:T(8,128)(2,1)S(1)}, bf16[16,2048]{1,0:T(8,128)(2,1)}, u32[]{:S(2)}) %copy-start) | copy-done | bytes 65560
  1.5 0.0 copy-start.1
  1.5 0.8 %copy-done.1 = bf16[16,2048]{1,0:T(8,128)(2,1)S(1)} copy-done((bf16[16,2048]{1,0:T(8,128)(2,1)S(1)}, bf16[16,2048]{1,0:T(8,128)(2,1)}, u32[]{:S(2)}) %copy-start.1) | copy-done | bytes 65560
  2.3 64.3 %shard_map.84 = (bf16[128,2048]{1,0:T(8,128)(2,1)S(1)}, bf16[128,2048]{1,0:T(8,128)(2,1)S(1)}, bf16[4,3,128,512]{3,2,1,0:T(8,128)(2,1)S(1)}, bf16[16,2048]{1,0:T(8,128)(2,1)S(1)}) custom-call(bf16[16,2048]{1,0:T(8,128)(2,1)S(1)} %copy-done, bf16[16,2048]{1,0:T(8,128)(2,1)S(1)} %copy-done.1, bf16[2048,2048]{1,0:T(8,128)(2,1)} %gw_hbm.1, ...), custom_call_target="tpu_custom_call" | custom-call | flops 5368709120 | bytes 25165824 | tf_op jit(solution)/shard_map/pallas_call | solution.py:227
  66.7 10.6 %shard_map.85 = (bf16[2048,2048]{1,0:T(8,128)(2,1)}, bf16[2048,2048]{1,0:T(8,128)(2,1)}, bf16[2048,2048]{1,0:T(8,128)(2,1)}) custom-call(bf16[128,2048]{1,0:T(8,128)(2,1)S(1)} %get-tuple-element.12.rows_ref, bf16[128,2048]{1,0:T(8,128)(2,1)S(1)} %get-tuple-element.13.grads_ref, bf16[4,3,128,512]{3,2,1,0:T(8,128)(2,1)S(1)} %get-tuple-element.14.res_ref.hid_ref, ...), custom_call_target="tpu_custom_call" | custom-call | flops 3221225472 | bytes 25165824 | tf_op jit(solution)/shard_map/pallas_call | solution.py:287
  77.2 0.6 copy.10
Async XLA Ops:
  0.6 0.8 %copy-start = (bf16[16,2048]{1,0:T(8,128)(2,1)S(1)}, bf16[16,2048]{1,0:T(8,128)(2,1)}, u32[]{:S(2)}) copy-start(bf16[16,2048]{1,0:T(8,128)(2,1)} %tok_ref.1) | copy-start | bytes 196612
  1.5 0.8 %copy-start.1 = (bf16[16,2048]{1,0:T(8,128)(2,1)S(1)}, bf16[16,2048]{1,0:T(8,128)(2,1)}, u32[]{:S(2)}) copy-start(bf16[16,2048]{1,0:T(8,128)(2,1)} %og_ref.1) | copy-start | bytes 196612

commit v2 on v1

--- a/solution.py
+++ b/solution.py
@@ -29,12 +29,15 @@
 def layer_kernel(
     nrow, ncol,
     tok_ref, og_ref, gw_hbm, uw_hbm, dw_hbm,
-    rows_hbm, grads_hbm, res_hbm, ig_ref,
-    gw, uw, dw, rows, grads, part, wide, inbox, res, tot, sib, pair, pbox,
-    w_sem, out_sem, g_send, g_recv, f_send, f_recv,
-    rs_send, rs_recv, ag_send, ag_recv, s_send, s_recv, p_send, p_recv,
+    rows_hbm, grads_hbm, res_hbm, own_ref, *more,
 ):
     nz = nrow // 2
+    pair_refs = more[: nz - 1]
+    (
+        gw, uw, dw, rows, grads, part, wide, inbox, res, tot, sib,
+        in_sem, w_sem, out_sem, g_send, g_recv, f_send, f_recv,
+        rs_send, rs_recv, ag_send, ag_recv, fw_send, fw_recv, s_send, s_recv,
+    ) = more[nz - 1 :]
     nc, d_loc, cw = gw.shape
     tb = tok_ref.shape[0]
     tc = rows.shape[0] // ncol
@@ -57,13 +60,17 @@
         src = dw_hbm.at[cols, :] if i == 2 else (gw_hbm, uw_hbm)[i].at[:, cols]
         return pltpu.make_async_copy(src, (gw, uw, dw)[i].at[c], w_sem.at[i, c])
 
+    own_tok = pltpu.make_async_copy(tok_ref, rows.at[block(r, tb), :], in_sem.at[0])
+    own_og = pltpu.make_async_copy(og_ref, grads.at[block(r, tb), :], in_sem.at[1])
+    own_tok.start()
+    own_og.start()
     for c in range(nc):
         weight_copy(0, c).start()
         weight_copy(1, c).start()
     for c in range(nc):
         weight_copy(2, c).start()
-    rows[block(r, tb), :] = tok_ref[...]
-    grads[block(r, tb), :] = og_ref[...]
+    own_tok.wait()
+    own_og.wait()
     pl.semaphore_wait(barrier, nz + ncol - 1)
 
     def gather_copy(a, k):
@@ -85,13 +92,15 @@
         for k in range(1, nz):
             gather_copy(a, k).wait_recv()
             forward_copy(a, k).start()
+        if a == 0:
+            for k in range(nz):
+                gather_copy(1, k).start()
         gather_copy(a, 0).wait_recv()
         for k in range(1, nz):
             forward_copy(a, k).wait_recv()
 
-    for a in range(2):
-        for k in range(nz):
-            gather_copy(a, k).start()
+    for k in range(nz):
+        gather_copy(0, k).start()
 
     def part_copy(c, kind, k):
         to = xor(me, k, ncol)
@@ -137,6 +146,23 @@
             mine, mine, ag_send.at[c, k - 1], ag_recv.at[c, k - 1],
             device_id={"col": xor(me, k, ncol)}, device_id_type=MESH,
         )
+
+    relayed = ncol == 4 and tc % 32 == 0
+    direct = (1, 2) if relayed else tuple(range(1, ncol))
+
+    def relay_copy(c, k):
+        half = pl.ds(pl.multiple_of(xor(me, k, ncol) * tc + (k - 1) * (tc // 2), tc // 2), tc // 2)
+        got = res.at[c, :, half, :]
+        return pltpu.make_async_remote_copy(
+            got, got, fw_send.at[c, k - 1], fw_recv.at[c, k - 1],
+            device_id={"col": xor(me, 3 - k, ncol)}, device_id_type=MESH,
+        )
+
+    def arrive(c):
+        for k in direct:
+            res_copy(c, k).wait_recv()
+            if relayed:
+                relay_copy(c, k).start()
 
     @pl.loop(0, nc)
     def _(c):
@@ -152,16 +178,23 @@
         res[c, 0, own, :] = (act * up).astype(BF16)
         res[c, 1, own, :] = (hidden_grad * up * sig * (1.0 + gate * (1.0 - sig))).astype(BF16)
         res[c, 2, own, :] = (hidden_grad * act).astype(BF16)
-        for k in range(1, ncol):
+        for k in direct:
             res_copy(c, k).start()
 
     td = min(512, d_loc)
     tot[...] = jnp.zeros_like(tot)
 
+    arrive(0)
+
     @pl.loop(0, nc)
     def _(c):
-        for k in range(1, ncol):
-            res_copy(c, k).wait_recv()
+        @pl.when(c + 1 < nc)
+        def _():
+            arrive(c + 1)
+
+        if relayed:
+            for k in (1, 2):
+                relay_copy(c, k).wait_recv()
         for j in range(d_loc // td):
             cut = pl.ds(j * td, td)
             tot[:, cut] += mm(res[c, 1], gw[c, cut, :], NT) + mm(res[c, 2], uw[c, cut, :], NT)
@@ -172,28 +205,16 @@
         return pltpu.make_async_remote_copy(
             tot.at[block(2 * k + 1 - core, tb), :], sib.at[k], s_send.at[k], s_recv.at[k],
             device_id={"row": sibling}, device_id_type=MESH,
-        )
-
-    def pair_copy(k):
-        to = xor(z, k, nz)
-        return pltpu.make_async_remote_copy(
-            pair.at[to], pbox.at[k - 1], p_send.at[k - 1], p_recv.at[k - 1],
-            device_id={"row": to * 2 + core}, device_id_type=MESH,
         )
 
     for k in range(nz):
         sib_copy(k).start()
     for k in range(nz):
         sib_copy(k).wait_recv()
-    for k in range(nz):
-        pair[k] = (tot[block(2 * k + core, tb), :] + sib[k]).astype(BF16)
+    own_ref[...] = tot[block(r, tb), :] + sib[z]
     for k in range(1, nz):
-        pair_copy(k).start()
-    total = tot[block(r, tb), :] + sib[z]
-    for k in range(1, nz):
-        pair_copy(k).wait_recv()
-        total = total + pbox[k - 1].astype(F32)
-    ig_ref[...] = total.astype(BF16)
+        to = xor(z, k, nz)
+        pair_refs[k - 1][...] = (tot[block(2 * to + core, tb), :] + sib[to]).astype(BF16)
 
     for a in range(2):
         for k in range(nz):
@@ -205,11 +226,12 @@
         def _(c):
             part_copy(c, 0, k).wait_send()
             part_copy(c, 1, k).wait_send()
-            res_copy(c, k).wait_send()
+            if k in direct:
+                res_copy(c, k).wait_send()
+            if relayed and k < 3:
+                relay_copy(c, k).wait_send()
     for k in range(nz):
         sib_copy(k).wait_send()
-    for k in range(1, nz):
-        pair_copy(k).wait_send()
     out_rows.wait()
     out_grads.wait()
     out_res.wait()
@@ -230,10 +252,11 @@
             jax.ShapeDtypeStruct((t, d_loc), BF16),
             jax.ShapeDtypeStruct((t, d_loc), BF16),
             jax.ShapeDtypeStruct((nc, 3, t, cw), BF16),
-            jax.ShapeDtypeStruct((tb, d_loc), BF16),
-        ),
-        in_specs=[vmem, vmem, hbm, hbm, hbm],
-        out_specs=(hbm, hbm, hbm, vmem),
+            jax.ShapeDtypeStruct((tb, d_loc), F32),
+            *[jax.ShapeDtypeStruct((tb, d_loc), BF16)] * (nz - 1),
+        ),
+        in_specs=[pl.BlockSpec(memory_space=pltpu.HBM)] * 5,
+        out_specs=(hbm, hbm, hbm) + (vmem,) * nz,
         scratch_shapes=[
             pltpu.VMEM((nc, d_loc, cw), BF16),
             pltpu.VMEM((nc, d_loc, cw), BF16),
@@ -246,13 +269,11 @@
             pltpu.VMEM((nc, 3, t, cw), BF16),
             pltpu.VMEM((t, d_loc), F32),
             pltpu.VMEM((nz, tb, d_loc), F32),
-            pltpu.VMEM((nz, tb, d_loc), BF16),
-            pltpu.VMEM((nz - 1, tb, d_loc), BF16),
-            dma((3, nc)), dma((3,)),
+            dma((2,)), dma((3, nc)), dma((3,)),
             dma((2, nz)), dma((2, nz)), dma((2, nz - 1)), dma((2, nz - 1)),
             dma((2, nc, ncol - 1)), dma((2, nc, ncol - 1)),
-            dma((nc, ncol - 1)), dma((nc, ncol - 1)),
-            dma((nz,)), dma((nz,)), dma((nz - 1,)), dma((nz - 1,)),
+            dma((nc, ncol - 1)), dma((nc, ncol - 1)), dma((nc, 2)), dma((nc, 2)),
+            dma((nz,)), dma((nz,)),
         ],
         compiler_params=pltpu.CompilerParams(
             collective_id=0, has_side_effects=True, vmem_limit_bytes=48 * 1024 * 1024
@@ -314,10 +335,17 @@
     nrow, ncol = mesh.shape["row"], mesh.shape["col"]
 
     def body(tokens, out_grad, gate_weight, up_weight, down_weight):
-        rows, grads, res, input_grad = layer(
+        rows, grads, res, total, *pairs = layer(
             nrow, ncol, tokens, out_grad, gate_weight, up_weight, down_weight
         )
-        return (input_grad, *weight_grads(rows, grads, res))
+        got = [
+            lax.ppermute(p, "row", [(r, (r // 2 ^ k) * 2 + r % 2) for r in range(nrow)])
+            for k, p in enumerate(pairs, 1)
+        ]
+        weights = weight_grads(rows, grads, res)
+        for p in got:
+            total = total + p.astype(F32)
+        return (total.astype(BF16), *weights)
 
     return jax.shard_map(
         body,

time: 78.1 us -> 70.7 us (0.905)
  Pallas kernels: 74.9 us -> 63 us
  starting transfers between devices: 0 us -> 4.49 us
    pallas_call x1, Pallas kernels: 64.3 us -> 52.4 us  [layer(): pl.pallas_call(functools.partial(layer_kernel, nrow, ncol), out_shape=(ja...]
    ppermute x0 -> x3, starting transfers between devices: none -> 4.49 us  [body(): lax.ppermute(p, 'row', [(r, (r // 2 ^ k) * 2 + r % 2) for r in range(nrow)])]
    unnamed x5 -> x4, local copies, waits for them, and re-layouts: 2.3 us -> 1.67 us
  transfers between devices with their start and end apart: 0 -> 3, of which waited for: 0 -> 0; matrix products, arithmetic and copies ran while one was open for 0% -> 0% of each run, Pallas kernels for 0% -> 15%
where the time goes in v2:
time: 70.7 us; the launch traced here: 70.5 us
  Pallas kernels  63 us (89%)
  starting transfers between devices  4.49 us (6%)
  local copies, waits for them, and re-layouts  1.67 us (2%)
    pallas_call x1, Pallas kernels, layer(): pl.pallas_call(functools.partial(layer_kernel, nrow, ncol), out_shape=(ja...  52.4 us
    pallas_call x1, Pallas kernels, weight_grads(): pl.pallas_call(grads_kernel, grid=(steps,), out_shape=(jax.ShapeDtypeStru...  10.5 us
    ppermute x3, starting transfers between devices, body(): lax.ppermute(p, 'row', [(r, (r // 2 ^ k) * 2 + r % 2) for r in range(nrow)])  4.49 us
    unnamed x4, local copies, waits for them, and re-layouts  1.67 us
  transfers between devices with their start and end apart: 3, of which 0 were waited for; matrix products, arithmetic and copies ran while one was open for 0% of the time, Pallas kernels for 15%

profile of v2, /device:TPU:0, one launch (start us, length us, event | category | flops | bytes accessed | tf_op | source)
XLA Modules:
  0.0 70.5 jit_solution(10388694377049789053)
XLA Ops:
  0.6 0.0 copy-start
  0.6 0.8 %copy-done = bf16[16,2048]{1,0:T(8,128)(2,1)S(1)} copy-done((bf16[16,2048]{1,0:T(8,128)(2,1)S(1)}, bf16[16,2048]{1,0:T(8,128)(2,1)}, u32[]{:S(2)}) %copy-start) | copy-done | bytes 65560
  1.5 0.0 copy-start.1
  1.5 0.8 %copy-done.1 = bf16[16,2048]{1,0:T(8,128)(2,1)S(1)} copy-done((bf16[16,2048]{1,0:T(8,128)(2,1)S(1)}, bf16[16,2048]{1,0:T(8,128)(2,1)}, u32[]{:S(2)}) %copy-start.1) | copy-done | bytes 65560
  2.3 52.4 %shard_map.84 = (bf16[128,2048]{1,0:T(8,128)(2,1)S(1)}, bf16[128,2048]{1,0:T(8,128)(2,1)S(1)}, bf16[4,3,128,512]{3,2,1,0:T(8,128)(2,1)S(1)}, f32[16,2048]{1,0:T(...) custom-call(bf16[16,2048]{1,0:T(8,128)(2,1)S(1)} %copy-done, ...), custom_call_target="tpu_custom_call" | custom-call | flops 5368709120 | bytes 25165824 | tf_op jit(solution)/shard_map/pallas_call | solution.py:249
  54.8 2.0 %collective-permute-start = (bf16[16,2048]{1,0:T(8,128)(2,1)S(1)}, bf16[16,2048]{1,0:T(8,128)(2,1)S(1)}, u32[]{:S(2)}, u32[]{:S(2)}) collective-permute-start(bf16[16,2048]{1,0:T(8,128)(2,1)S(1)} %get-tuple-element.15), channel_id=1, source_target_pairs={{0,8},{4,12},{8,0},{12,4},{16,24},{20,28},{24,16},{28,20},{1,9},{5... | collective-permute-start | bytes 196616 | tf_op jit(solution)/shard_map/ppermute | solution.py:342
  56.8 1.0 %collective-permute-start.1 = (bf16[16,2048]{1,0:T(8,128)(2,1)S(1)}, bf16[16,2048]{1,0:T(8,128)(2,1)S(1)}, u32[]{:S(2)}, u32[]{:S(2)}) collective-permute-start(bf16[16,2048]{1,0:T(8,128)(2,1)S(1)} %get-tuple-element.16), channel_id=1, source_target_pairs={{0,16},{4,20},{8,24},{12,28},{16,0},{20,4},{24,8},{28,12},{1,17},{... | collective-permute-start | bytes 196616 | tf_op jit(solution)/shard_map/ppermute | solution.py:342
  57.8 1.4 %collective-permute-start.2 = (bf16[16,2048]{1,0:T(8,128)(2,1)S(1)}, bf16[16,2048]{1,0:T(8,128)(2,1)S(1)}, u32[]{:S(2)}, u32[]{:S(2)}) collective-permute-start(bf16[16,2048]{1,0:T(8,128)(2,1)S(1)} %get-tuple-element.17), channel_id=1, source_target_pairs={{0,24},{4,28},{8,16},{12,20},{16,8},{20,12},{24,0},{28,4},{1,25},{... | collective-permute-start | bytes 196616 | tf_op jit(solution)/shard_map/ppermute | solution.py:342
  59.3 10.5 %shard_map.85 = (bf16[2048,2048]{1,0:T(8,128)(2,1)}, bf16[2048,2048]{1,0:T(8,128)(2,1)}, bf16[2048,2048]{1,0:T(8,128)(2,1)}) custom-call(bf16[128,2048]{1,0:T(8,128)(2,1)S(1)} %get-tuple-element.18.rows_ref, bf16[128,2048]{1,0:T(8,128)(2,1)S(1)} %get-tuple-element.19.grads_ref, bf16[4,3,128,512]{3,2,1,0:T(8,128)(2,1)S(1)} %get-tuple-element.20.res_ref.hid_ref, ...), custom_call_target="tpu_custom_call" | custom-call | flops 3221225472 | bytes 25165824 | tf_op jit(solution)/shard_map/pallas_call | solution.py:308
  69.8 0.0 collective-permute-done
  69.8 0.0 collective-permute-done.1
  69.8 0.0 collective-permute-done.2
  69.8 0.7 add_convert_fusion
Async XLA Ops:
  0.6 0.8 %copy-start = (bf16[16,2048]{1,0:T(8,128)(2,1)S(1)}, bf16[16,2048]{1,0:T(8,128)(2,1)}, u32[]{:S(2)}) copy-start(bf16[16,2048]{1,0:T(8,128)(2,1)} %tok_ref.1) | copy-start | bytes 196612
  1.5 0.8 %copy-start.1 = (bf16[16,2048]{1,0:T(8,128)(2,1)S(1)}, bf16[16,2048]{1,0:T(8,128)(2,1)}, u32[]{:S(2)}) copy-start(bf16[16,2048]{1,0:T(8,128)(2,1)} %og_ref.1) | copy-start | bytes 196612
  54.8 15.0 %collective-permute-start = (bf16[16,2048]{1,0:T(8,128)(2,1)S(1)}, bf16[16,2048]{1,0:T(8,128)(2,1)S(1)}, u32[]{:S(2)}, u32[]{:S(2)}) collective-permute-start(bf16[16,2048]{1,0:T(8,128)(2,1)S(1)} %get-tuple-element.15), channel_id=1, source_target_pairs={{0,8},{4,12},{8,0},{12,4},{16,24},{20,28},{24,16},{28,20},{1,9},{5... | collective-permute-start | bytes 196616 | tf_op jit(solution)/shard_map/ppermute | solution.py:342
  56.8 13.0 %collective-permute-start.1 = (bf16[16,2048]{1,0:T(8,128)(2,1)S(1)}, bf16[16,2048]{1,0:T(8,128)(2,1)S(1)}, u32[]{:S(2)}, u32[]{:S(2)}) collective-permute-start(bf16[16,2048]{1,0:T(8,128)(2,1)S(1)} %get-tuple-element.16), channel_id=1, source_target_pairs={{0,16},{4,20},{8,24},{12,28},{16,0},{20,4},{24,8},{28,12},{1,17},{... | collective-permute-start | bytes 196616 | tf_op jit(solution)/shard_map/ppermute | solution.py:342
  57.8 12.0 %collective-permute-start.2 = (bf16[16,2048]{1,0:T(8,128)(2,1)S(1)}, bf16[16,2048]{1,0:T(8,128)(2,1)S(1)}, u32[]{:S(2)}, u32[]{:S(2)}) collective-permute-start(bf16[16,2048]{1,0:T(8,128)(2,1)S(1)} %get-tuple-element.17), channel_id=1, source_target_pairs={{0,24},{4,28},{8,16},{12,20},{16,8},{20,12},{24,0},{28,4},{1,25},{... | collective-permute-start | bytes 196616 | tf_op jit(solution)/shard_map/ppermute | solution.py:342
